TPU v7x, 256 devices: a whole 4x4x8 slice. The times are simulated.
256 devices in a mesh: dp: 16 (over y, x_lo, core), cent: 16 (over x_hi, z).
Axes of the slice: x: 4 (x_hi: 2, x_lo: 2; x = x_hi * 2 + x_lo), y: 4, z: 8, core: 2. Of those that a mesh axis runs over, the one named last changes fastest.
Arguments:
- vectors: bfloat16 [524288, 1024], P(('dp', 'cent'))
- centroids: bfloat16 [1024, 1024], P('cent')
Outputs:
- updated: float32 [1024, 1024], P('cent', 'dp')
All inputs are finite; a program needn't handle non-finite values.
Results may differ from a plain program's by a relative error of at most 0.0011.
Values may be sent and summed in bfloat16 or wider, within the bound.
A program may use at most 64 MiB of HBM per device.

v0:
```python
import math

import jax
import jax.numpy as jnp
from jax import lax
from jax.sharding import PartitionSpec as P


def logit_block(vectors, panel_rows):
    norms = jnp.sum(panel_rows.astype(jnp.float32) ** 2, axis=1)
    cross = lax.dot_general(
        vectors, panel_rows, (((1,), (1,)), ((), ())), preferred_element_type=jnp.float32
    )
    return (2.0 * cross - norms[None, :]) / math.sqrt(vectors.shape[1])


def per_device(vectors, centroids):
    row_count = vectors.shape[0]
    feature_count = vectors.shape[1]
    panel_count = centroids.shape[0]
    logits = logit_block(vectors, lax.all_gather(centroids, "cent", axis=0, tiled=True))
    row_top = jnp.max(logits, axis=1, keepdims=True)
    lse = row_top + jnp.log(jnp.sum(jnp.exp(logits - row_top), axis=1, keepdims=True))
    resp = jnp.exp(logits - lse).astype(jnp.bfloat16)
    ones_row = jnp.ones((1, row_count), jnp.bfloat16)
    local_weights = jnp.dot(ones_row, resp, preferred_element_type=jnp.float32)[0]
    weight_sums = lax.psum(local_weights, ("dp", "cent"))
    shard_width = feature_count // lax.axis_size("dp")
    panel_numer = lax.psum_scatter(
        lax.dot_general(
            resp, vectors, (((0,), (0,)), ((), ())), preferred_element_type=jnp.float32
        ),
        "cent",
        scatter_dimension=0,
        tiled=True,
    )
    mine = lax.psum_scatter(panel_numer, "dp", scatter_dimension=1, tiled=True)
    own_block = lax.dynamic_slice_in_dim(
        centroids, lax.axis_index("dp") * shard_width, shard_width, 1
    ).astype(jnp.float32)
    own_weights = lax.dynamic_slice_in_dim(
        weight_sums, lax.axis_index("cent") * panel_count, panel_count, 0
    )
    return (mine + own_block) / (own_weights[:, None] + 1.0)


def solution(mesh):
    in_specs = (P(("dp", "cent"), None), P("cent", None))
    out_specs = P("cent", "dp")
    return jax.shard_map(
        per_device, mesh=mesh, in_specs=in_specs, out_specs=out_specs, check_vma=False
    )
```

profile of v0, /device:TPU:1, one launch (start us, length us, event | category | flops | bytes accessed | tf_op | source)
XLA Modules:
  0.0 415.5 jit_solution(16121253305223933986)
XLA Ops:
  6.5 0.0 all-gather.2.cloned.1.call-start
  6.5 0.7 all-gather.2.cloned.1.call-update
  7.3 0.0 reduce-scatter.5.cloned.1.call-start
  7.3 88.4 %all-gather.2.cloned.1.call-done = bf16[1024,1024]{1,0:T(8,128)(2,1)} async-done(((bf16[64,1024]{1,0:T(8,128)(2,1)}), bf16[1024,1024]{1,0:T(8,128)(2,1)}) %all-gather.2.cloned.1.call-update) | async-done | bytes 2097168 | tf_op jit(solution)/shard_map/all_gather | solution.py:21
  95.7 2.1 multiply_reduce_fusion
  97.7 7.1 %fusion = (f32[2048]{0:T(1024)S(1)}, f32[2048,1024]{0,1:T(8,128)S(1)}) fusion(f32[1024]{0:T(1024)S(1)} %multiply_reduce_fusion, bf16[2048,1024]{1,0:T(8,128)(2,1)} %param.2, bf16[1024,1024]{1,0:T(8,128)(2,1)} %all-gather.2.cloned.1.call-done), kind=kOutput, calls=%fused_computation.3 | convolution fusion | flops 4303353856 | bytes 14692352 | tf_op jit(solution)/shard_map/dot_general | solution.py:11
  104.8 2.5 exponential_reduce_fusion
  107.3 0.0 copy-start.1
  107.3 2.5 exponential_convert_fusion
  109.8 0.0 copy-start
  109.8 1.9 copy-done
  111.8 0.0 copy-done.1
  111.8 6.0 %fusion.4 = f32[1024,1024]{1,0:T(8,128)} fusion(bf16[2048,1024]{0,1:T(8,128)(2,1)S(1)} %exponential_convert_fusion, bf16[2048,1024]{1,0:T(8,128)(2,1)S(1)} %copy-done.1), kind=kOutput, calls=%fused_computation.11 | convolution fusion | flops 4294967296 | bytes 12582912 | tf_op jit(solution)/shard_map/dot_general | solution.py:30
  117.8 0.0 reduce-scatter.5.cloned.1.call-update
  117.8 0.0 reduce-scatter.7.cloned.1.call-start
  117.9 204.5 %reduce-scatter.5.cloned.1.call-done = f32[64,1024]{1,0:T(8,128)} async-done(((f32[1024,1024]{1,0:T(8,128)}), f32[64,1024]{1,0:T(8,128)}) %reduce-scatter.5.cloned.1.call-update) | async-done | bytes 262160 | tf_op jit(solution)/shard_map/reduce_scatter | solution.py:29
  322.4 1.9 copy.3
  324.3 0.0 reduce-scatter.7.cloned.1.call-update
  324.4 3.4 fusion.1
  327.7 78.9 %psum.7 = f32[1024]{0:T(1024)S(1)} all-reduce(f32[1024]{0:T(1024)S(1)} %bitcast.10), channel_id=1, replica_groups=mesh['dp'=16,'cent'=16] {'dp','cent'}, use_global_device_ids=true, to_apply=%region_5.0 | all-reduce | flops 1024 | bytes 8192 | tf_op jit(solution)/shard_map/psum | solution.py:27
  406.6 0.1 dynamic-slice_add_fusion
  406.7 0.0 reduce-scatter.7.cloned.1.call-done
  406.7 0.8 copy.4
  407.5 1.4 add_divide_fusion
  (1 shorter events, 0.0 us)
Async XLA Ops:
  6.5 89.1 %all-gather.2.cloned.1.call-start = ((), (), s32[]{:S(2)}) async-start(), calls=%async_computation.2 | async-start | bytes 2228224 | tf_op jit(solution)/shard_map/all_gather | solution.py:21
  7.3 315.1 %reduce-scatter.5.cloned.1.call-start = ((), (), s32[]{:S(2)}) async-start(), calls=%async_computation.3 | async-start | bytes 4456448 | tf_op jit(solution)/shard_map/reduce_scatter | solution.py:29
  107.3 4.5 %copy-start.1 = (bf16[2048,1024]{1,0:T(8,128)(2,1)S(1)}, bf16[2048,1024]{1,0:T(8,128)(2,1)}, u32[]{:S(2)}) copy-start(bf16[2048,1024]{1,0:T(8,128)(2,1)} %param.2) | copy-start | bytes 12582916
  109.8 1.9 copy-start
  117.8 288.8 %reduce-scatter.7.cloned.1.call-start = ((), (), s32[]{:S(2)}) async-start(), calls=%async_computation.4 | async-start | bytes 557056
Sparse Core Ops, SparseCore 0:
  9.9 85.6 all-gather.1
  118.0 204.3 reduce-scatter.4
  325.0 62.4 reduce-scatter.6
where the time goes:
time: 416 us; the launch traced here: 415 us
  waiting for transfers between devices  294 us (71%)
  blocking collectives  78.9 us (19%)
  matrix products  16.5 us (4%)
  between operations  13.2 us (3%)
  other arithmetic  8.55 us (2%)
  local copies, waits for them, and re-layouts  4.7 us (1%)
    reduce_scatter x1, waiting for transfers between devices, per_device(): lax.psum_scatter(lax.dot_general(resp, vectors, (((0,), (0,)), ((), ())),...  205 us
    all_gather x1, waiting for transfers between devices, per_device(): lax.all_gather(centroids, 'cent', axis=0, tiled=True)  88.4 us
    psum x1, blocking collectives, per_device(): weight_sums = lax.psum(local_weights, ('dp', 'cent'))  78.9 us
  transfers between devices with their start and end apart: 3, of which 2 were waited for; matrix products, arithmetic and copies ran while one was open for 1% of the time, Pallas kernels for 0%

commit v1 on v0

v1 whole, which is shorter than its diff:
```python
import functools
import math

import jax
import jax.numpy as jnp
from jax import lax
from jax.experimental import pallas as pl
from jax.experimental.pallas import tpu as pltpu
from jax.sharding import PartitionSpec as P

F32 = jnp.float32
BF16 = jnp.bfloat16
LOG2E = math.log2(math.e)
DZ = (0, 1, 7, 2, 6, 3, 5, 4)
NT = (((1,), (1,)), ((), ()))


def device(x, y, z, core):
    return {"dp": y * 4 + lax.rem(x, 2) * 2 + core, "cent": (x // 2) * 8 + z}


def kernel(
    vec_hbm, cen, out,
    vec, G, E, R, ms, ss, wp, NUM, SIB, RSIB, SB, RB, S2, R2, S3, R3,
    W0, W1, W2, WS, WA, WB, WZ,
    load_sem, gs, gr, fs, fr, hs, hr, cs, cr, a_s, a_r, b_s, b_r, zs, zr, ws, wr,
):
    dp, cent = lax.axis_index("dp"), lax.axis_index("cent")
    core = lax.rem(dp, 2)
    x_lo = lax.rem(dp // 2, 2)
    y = dp // 4
    xh = cent // 8
    z = lax.rem(cent, 8)
    x = xh * 2 + x_lo
    first = core == 0
    sibling = device(x, y, z, 1 - core)

    def on_x(j):
        return device(lax.rem(x + j, 4), y, z, core)

    def on_y(j):
        return device(x, lax.rem(y + j, 4), z, core)

    def on_z(j):
        return device(x, y, lax.rem(z + j, 8), core)

    def on_a(j):
        return device(lax.rem(x + j * core, 4), lax.rem(y + j * (1 - core), 4), z, core)

    def on_b(j):
        return device(lax.rem(x + j * (1 - core), 4), lax.rem(y + j * core, 4), z, core)

    load = pltpu.make_async_copy(vec_hbm, vec, load_sem)
    load.start()

    barrier = pltpu.get_barrier_semaphore()
    peers = [sibling]
    peers += [on_x(j) for j in (1, 2, 3)]
    peers += [on_y(j) for j in (1, 2, 3)]
    peers += [on_z(j) for j in range(1, 8)]
    for peer in peers:
        pl.semaphore_signal(barrier, inc=1, device_id=peer)

    h = x_lo + xh - 2 * x_lo * xh
    quarter = lax.rem(y + 2 * h, 4)
    cols = pl.ds(pl.multiple_of(core * 512, 512), 512)
    G[quarter, 0, xh, :, cols] = cen[pl.ds(pl.multiple_of(quarter * 16, 16), 16), cols]

    pl.semaphore_wait(barrier, len(peers))

    sent = []

    def send(src, dst, s, r, to):
        copy = pltpu.make_async_remote_copy(
            src_ref=src, dst_ref=dst, send_sem=s, recv_sem=r, device_id=to
        )
        copy.start()
        sent.append(copy)
        return copy

    across = device(3 - x, y, z, core)
    beside = device(x + 1 - 2 * x_lo, y, z, core)
    own = G.at[quarter, 0, xh, :, cols]
    to_across = send(own, own, gs.at[14], gr.at[14], across)
    ring = [
        send(own, G.at[quarter, s, xh, :, cols], gs.at[s - 1], gr.at[s - 1], on_z(8 - DZ[s]))
        for s in range(1, 8)
    ]
    to_across.wait_recv()
    other = G.at[quarter, 0, 1 - xh, :, cols]
    ring2 = [
        send(other, G.at[quarter, s, 1 - xh, :, cols], gs.at[6 + s], gr.at[6 + s], on_z(8 - DZ[s]))
        for s in range(1, 8)
    ]
    near = (on_y(1), on_y(3), beside, sibling)
    passed = []
    for s in range(8):
        if s:
            ring[s - 1].wait_recv()
            ring2[s - 1].wait_recv()
        piece = G.at[quarter, s, :, :, cols]
        passed.append(
            [send(piece, piece, fs.at[s * 4 + k], fr.at[s * 4 + k], near[k]) for k in range(4)]
        )

    def logits(q):
        g = G[q].reshape(256, 1024)
        gf = g.astype(F32)
        bias = jnp.sum(gf * gf, axis=1, keepdims=True) * (LOG2E / 32.0)

        def body(i, carry):
            for u in range(4):
                n = pl.ds(pl.multiple_of(i * 1024 + u * 256, 256), 256)
                cross = lax.dot_general(g, vec[n, :], NT, preferred_element_type=F32)
                logit = cross * (LOG2E / 16.0) - bias
                top = jnp.max(logit, axis=0, keepdims=True)
                e = jnp.exp2(logit - top)
                E[q, :, n] = e
                ms[q, :, n] = top
                ss[q, :, n] = jnp.sum(e, axis=0, keepdims=True)
            return carry

        lax.fori_loop(0, 2, body, 0)

    load.wait()
    for s in range(8):
        passed[s][3].wait_recv()
    logits(quarter)
    quarters = (lax.rem(quarter + 3, 4), lax.rem(quarter + 1, 4), lax.rem(quarter + 2, 4))
    over = []
    for k in range(3):
        for s in range(8):
            passed[s][k].wait_recv()
        piece = G.at[quarters[k], :, :, :, cols]
        over.append(send(piece, piece, hs.at[k], hr.at[k], sibling))
    for k in range(3):
        over[k].wait_recv()
        logits(quarters[k])

    tops = [ms[q] for q in range(4)]
    top = functools.reduce(jnp.maximum, tops)
    scales = [jnp.exp2(t - top) for t in tops]
    total = functools.reduce(jnp.add, [ss[q] * scales[q] for q in range(4)])
    for q in range(4):
        ms[q] = scales[q] / total

    def responsibilities(q, u):
        n = slice(u * 512, u * 512 + 512)
        r = (E[q, :, n] * ms[q, :, n]).astype(BF16)
        R[q, :, n] = r
        rf = r.astype(F32)
        part = rf[:, 0:128] + rf[:, 128:256] + rf[:, 256:384] + rf[:, 384:512]
        wp[q] = part if u == 0 else wp[q] + part

    lo = lax.broadcasted_iota(jnp.int32, (64, 128), 1) < 64

    def combine(q):
        to_sib[q].wait_recv()
        for xx in range(4):
            for yy in range(4):
                t = NUM[q, xx * 4 + yy] + RSIB[q, xx * 4 + yy]
                NUM[q, xx * 4 + yy] = t
                SB[q, jnp.where(first, yy, xx), jnp.where(first, xx, yy)] = t.astype(BF16)
        a = jnp.where(first, y, x)
        to_a.append(
            [
                send(SB.at[q, lax.rem(a + j, 4)], RB.at[q, j - 1], a_s.at[q * 3 + j - 1], a_r.at[q * 3 + j - 1], on_a(j))
                for j in (1, 2, 3)
            ]
        )

    to_sib, to_a = [], []
    for u in range(4):
        responsibilities(0, u)
    for q in range(4):
        for yy in range(4):
            d = jnp.dot(R[q], vec[:, yy * 256 : yy * 256 + 256], preferred_element_type=F32)
            if q < 3:
                responsibilities(q + 1, yy)
            d = d.reshape(8, 2, 2, 8, 256)
            for xx in range(4):
                lanes = slice((xx % 2) * 128, (xx % 2) * 128 + 128)
                top_rows = d[:, xx // 2, 0, :, lanes].reshape(64, 128)
                low_rows = d[:, xx // 2, 1, :, lanes].reshape(64, 128)
                p0 = jnp.where(lo, top_rows, pltpu.roll(low_rows, 64, 1))
                p1 = jnp.where(lo, pltpu.roll(top_rows, 64, 1), low_rows)
                NUM[q, xx * 4 + yy] = jnp.where(first, p0, p1)
                SIB[q, xx * 4 + yy] = jnp.where(first, p1, p0)
        to_sib.append(send(SIB.at[q], RSIB.at[q], cs.at[q], cr.at[q], sibling))
        if q >= 1:
            combine(q - 1)
        if q == 2:
            for k in range(8):
                block = wp[k // 2, (k % 2) * 128 : (k % 2) * 128 + 128, :]
                W0[k : k + 1, :] = jnp.sum(block.T, axis=0, keepdims=True)
            w_sib = send(W0, WS, ws.at[0], wr.at[0], sibling)
    w_sib.wait_recv()
    W1[...] = W0[...] + WS[...]
    w_a = [send(W1, WA.at[j - 1], ws.at[j], wr.at[j], on_a(j)) for j in (1, 2, 3)]
    combine(3)

    to_b = []
    b = jnp.where(first, x, y)
    for q in range(4):
        for j in range(3):
            to_a[q][j].wait_recv()
        for i in range(4):
            mine = NUM[q, jnp.where(first, i * 4 + y, x * 4 + i)]
            S2[q, i] = (
                mine + RB[q, 0, i].astype(F32) + RB[q, 1, i].astype(F32) + RB[q, 2, i].astype(F32)
            )
        to_b.append(
            [
                send(S2.at[q, lax.rem(b + j, 4)], R2.at[q, j - 1], b_s.at[q * 3 + j - 1], b_r.at[q * 3 + j - 1], on_b(j))
                for j in (1, 2, 3)
            ]
        )
        if q == 0:
            for j in range(3):
                w_a[j].wait_recv()
            W2[...] = W1[...] + WA[0] + WA[1] + WA[2]
            w_b = [send(W2, WB.at[j - 1], ws.at[3 + j], wr.at[3 + j], on_b(j)) for j in (1, 2, 3)]
    for j in range(3):
        w_b[j].wait_recv()
    W1b = W2[...] + WB[0] + WB[1] + WB[2]
    W0b = WS
    W0b[...] = W1b
    w_z = [send(W0b, WZ.at[s - 1], ws.at[6 + s], wr.at[6 + s], on_z(DZ[s])) for s in range(1, 8)]
    for q in range(4):
        for j in range(3):
            to_b[q][j].wait_recv()
        S3[q] = (S2[q, b] + R2[q, 0] + R2[q, 1] + R2[q, 2]).reshape(8, 8, 128)
    to_z = [
        send(S3.at[:, s], R3.at[s - 1], zs.at[s - 1], zr.at[s - 1], on_z(DZ[s])) for s in range(1, 8)
    ]
    for s in range(1, 8):
        w_z[s - 1].wait_recv()
    halves = [W0b[...], jnp.zeros((8, 128), F32)]
    for s in range(1, 8):
        w = WZ[s - 1]
        if s % 4:
            w = pltpu.roll(w, 128 - (s % 4) * 32, 1)
        halves[s // 4] = halves[s // 4] + w
    row = lax.broadcasted_iota(jnp.int32, (16, 128), 0)
    lane = lax.broadcasted_iota(jnp.int32, (16, 128), 1)
    mask = lane == row + xh * 16
    tile = pl.ds(pl.multiple_of((y * 2 + x_lo) * 128, 128), 128)
    block = cen[:, tile].astype(F32)
    block = jnp.where(first, block, pltpu.roll(block, 64, 1))
    for s in range(1, 8):
        to_z[s - 1].wait_recv()
    for q in range(4):
        w = halves[0][2 * q : 2 * q + 1, :] + halves[1][2 * q + 1 : 2 * q + 2, :]
        w = jnp.sum(jnp.where(mask, jnp.broadcast_to(w, (16, 128)), 0.0), axis=1, keepdims=True)
        f = S3[q, 0]
        for s in range(7):
            f = f + R3[s, q]
        rows = jnp.concatenate([f, pltpu.roll(f, 64, 1)], axis=0)
        res = (rows + block[q * 16 : q * 16 + 16]) / (w + 1.0)
        out[q * 16 : q * 16 + 16, :] = res[:, 0:64]
    for copy in sent:
        copy.wait_send()


def per_device(vectors, centroids):
    dma = pltpu.SemaphoreType.DMA
    vmem = pltpu.VMEM
    return pl.pallas_call(
        kernel,
        out_shape=jax.ShapeDtypeStruct((64, 64), F32),
        in_specs=[pl.BlockSpec(memory_space=pl.ANY), pl.BlockSpec(memory_space=pltpu.VMEM)],
        out_specs=pl.BlockSpec(memory_space=pltpu.VMEM),
        scratch_shapes=[
            vmem((2048, 1024), BF16),
            vmem((4, 8, 2, 16, 1024), BF16),
            vmem((4, 256, 2048), F32),
            vmem((4, 256, 2048), BF16),
            vmem((4, 1, 2048), F32),
            vmem((4, 1, 2048), F32),
            vmem((4, 256, 128), F32),
            vmem((4, 16, 64, 128), F32),
            vmem((4, 16, 64, 128), F32),
            vmem((4, 16, 64, 128), F32),
            vmem((4, 4, 4, 64, 128), BF16),
            vmem((4, 3, 4, 64, 128), BF16),
            vmem((4, 4, 64, 128), F32),
            vmem((4, 3, 64, 128), F32),
            vmem((4, 8, 8, 128), F32),
            vmem((7, 4, 8, 128), F32),
            vmem((8, 128), F32),
            vmem((8, 128), F32),
            vmem((8, 128), F32),
            vmem((8, 128), F32),
            vmem((3, 8, 128), F32),
            vmem((3, 8, 128), F32),
            vmem((7, 8, 128), F32),
            dma,
            dma((15,)), dma((15,)),
            dma((32,)), dma((32,)),
            dma((3,)), dma((3,)),
            dma((4,)), dma((4,)),
            dma((12,)), dma((12,)),
            dma((12,)), dma((12,)),
            dma((7,)), dma((7,)),
            dma((14,)), dma((14,)),
        ],
        compiler_params=pltpu.CompilerParams(
            collective_id=0, has_side_effects=True, vmem_limit_bytes=56 * 2**20
        ),
        name="step",
    )(vectors, centroids)


def solution(mesh):
    in_specs = (P(("dp", "cent"), None), P("cent", None))
    out_specs = P("cent", "dp")
    return jax.shard_map(
        per_device, mesh=mesh, in_specs=in_specs, out_specs=out_specs, check_vma=False
    )
```

time: 416 us -> 56.6 us (0.14)
  waiting for transfers between devices: 294 us -> 0 us
  blocking collectives: 78.9 us -> 0 us
  Pallas kernels: 0 us -> 55 us
  matrix products: 16.5 us -> 0 us
  between operations: 13.2 us -> 0.01 us
  other arithmetic: 8.55 us -> 0 us
    reduce_scatter x1 -> x0, waiting for transfers between devices: 205 us -> none  [per_device(): lax.psum_scatter(lax.dot_general(resp, vectors, (((0,), (0,)), ((), ())),...]
    all_gather x1 -> x0, waiting for transfers between devices: 88.4 us -> none  [per_device(): lax.all_gather(centroids, 'cent', axis=0, tiled=True)]
    psum x1 -> x0, blocking collectives: 78.9 us -> none  [per_device(): weight_sums = lax.psum(local_weights, ('dp', 'cent'))]
    pallas_call x0 -> x1, Pallas kernels: none -> 55 us  [per_device(): pl.pallas_call(kernel, out_shape=jax.ShapeDtypeStruct((64, 64), F32), in_...]
    dot_general x3 -> x0, matrix products: 16.5 us -> none  [the longest x1 7.06 us: logit_block(): lax.dot_general(vectors, panel_rows, (((1,), (1,)), ((), ())), preferred_...]
    reduce_sum x2 -> x0, other arithmetic: 4.56 us -> none  [the longest x1 2.49 us: per_device(): jnp.sum(jnp.exp(logits - row_top), axis=1, keepdims=True)]
  transfers between devices with their start and end apart: 3 -> 0, of which waited for: 2 -> 0; matrix products, arithmetic and copies ran while one was open for 1% -> 0% of each run, Pallas kernels for 0% -> 0%
where the time goes in v1:
time: 56.6 us; the launch traced here: 56.3 us
  Pallas kernels  55 us (97%)
  local copies, waits for them, and re-layouts  1.38 us (2%)
    pallas_call x1, Pallas kernels, per_device(): pl.pallas_call(kernel, out_shape=jax.ShapeDtypeStruct((64, 64), F32), in_...  55 us
    unnamed x1, local copies, waits for them, and re-layouts  1.38 us

profile of v1, /device:TPU:1, one launch (start us, length us, event | category | flops | bytes accessed | tf_op | source)
XLA Modules:
  0.0 56.3 jit_solution(1575252486313126732)
XLA Ops:
  0.0 55.0 %step.1 = f32[64,64]{1,0:T(8,128)} custom-call(bf16[2048,1024]{1,0:T(8,128)(2,1)} %vec_hbm.1, bf16[64,1024]{1,0:T(8,128)(2,1)} %cen.1), custom_call_target="tpu_custom_call" | custom-call | tf_op jit(solution)/shard_map/step/pallas_call | solution.py:268
  55.0 1.4 %copy.4 = f32[64,64]{1,0:T(8,128)} copy(f32[64,64]{1,0:T(8,128)} %step.1) | data formatting | bytes 32768

commit v2 on v1

v2 whole, which is shorter than its diff:
```python
import functools
import math

import jax
import jax.numpy as jnp
from jax import lax
from jax.experimental import pallas as pl
from jax.experimental.pallas import tpu as pltpu
from jax.sharding import PartitionSpec as P

F32 = jnp.float32
BF16 = jnp.bfloat16
LOG2E = math.log2(math.e)
NT = (((1,), (1,)), ((), ()))


def device(x, y, z, core):
    return {"dp": y * 4 + lax.rem(x, 2) * 2 + core, "cent": (x // 2) * 8 + z}


def each(lo, hi, step):
    def body(i, carry):
        step(i)
        return carry

    lax.fori_loop(lo, hi, body, 0)


def kernel(
    vec_hbm, cen_hbm, out,
    vec, cen, G, E, R, ms, ss, wp, NUM, SIB, RSIB, SB, RB, S2, SB2, R2, S3, R3,
    W0, W1, W2, W3, WS, WA, WB, WZ,
    load_sem, gs, gr, fs, fr, hs, hr, cs, cr, a_s, a_r, b_s, b_r, zs, zr, ws, wr,
):
    dp, cent = lax.axis_index("dp"), lax.axis_index("cent")
    core = lax.rem(dp, 2)
    x_lo = lax.rem(dp // 2, 2)
    y = dp // 4
    xh = cent // 8
    z = lax.rem(cent, 8)
    x = xh * 2 + x_lo
    first = core == 0
    sibling = device(x, y, z, 1 - core)

    def on_x(j):
        return device(lax.rem(x + j, 4), y, z, core)

    def on_y(j):
        return device(x, lax.rem(y + j, 4), z, core)

    def on_z(j):
        return device(x, y, lax.rem(z + j, 8), core)

    def on_a(j):
        return device(lax.rem(x + j * core, 4), lax.rem(y + j * (1 - core), 4), z, core)

    def on_b(j):
        return device(lax.rem(x + j * (1 - core), 4), lax.rem(y + j * core, 4), z, core)

    def distance(s):
        return jnp.where(lax.rem(s, 2) == 1, (s + 1) // 2, 8 - s // 2)

    def remote(src, dst, s, r, n, to):
        return pltpu.make_async_remote_copy(
            src_ref=src, dst_ref=dst, send_sem=s.at[n], recv_sem=r.at[n], device_id=to
        )

    barrier = pltpu.get_barrier_semaphore()
    peers = [sibling]
    peers += [on_x(j) for j in (1, 2, 3)]
    peers += [on_y(j) for j in (1, 2, 3)]
    peers += [on_z(j) for j in range(1, 8)]
    for peer in peers:
        pl.semaphore_signal(barrier, inc=1, device_id=peer)

    h = x_lo + xh - 2 * x_lo * xh
    quarter = lax.rem(y + 2 * h, 4)
    cols = pl.ds(pl.multiple_of(core * 512, 512), 512)
    own = cen_hbm.at[pl.ds(pl.multiple_of(quarter * 16, 16), 16), cols]
    place = pltpu.make_async_copy(own, G.at[xh, quarter, 0, :, cols], load_sem.at[0])
    place.start()
    load = pltpu.make_async_copy(vec_hbm, vec, load_sem.at[1])
    load.start()
    load_cen = pltpu.make_async_copy(cen_hbm, cen, load_sem.at[2])
    load_cen.start()
    place.wait()

    pl.semaphore_wait(barrier, len(peers))

    across = device(3 - x, y, z, core)
    near = (on_y(1), on_y(3), device(x + 1 - 2 * x_lo, y, z, core), sibling)
    quarters = (lax.rem(quarter + 3, 4), lax.rem(quarter + 1, 4), lax.rem(quarter + 2, 4))

    def piece(c, q, s):
        return G.at[xh + c * (1 - 2 * xh), q, s, :, cols]

    def ring(s):
        return remote(piece(0, quarter, 0), piece(0, quarter, s), gs, gr, s, on_z(8 - distance(s)))

    def cross(s):
        p = piece(0, quarter, s)
        return remote(p, p, gs, gr, 8 + s, across)

    def give(c, s, k):
        p = piece(c, quarter, s)
        return remote(p, p, fs, fr, c * 32 + s * 4 + k, near[k])

    def over(c, s, k):
        p = piece(c, quarters[k], s)
        return remote(p, p, hs, hr, c * 24 + s * 3 + k, sibling)

    def hop(s):
        ring(s).wait_recv()
        cross(s).start()
        for k in range(4):
            give(0, s, k).start()

    def forward(s):
        cross(s).wait_recv()
        for k in range(4):
            give(1, s, k).start()

    def share(c, s):
        for k in range(3):
            give(c, s, k).wait_recv()
            over(c, s, k).start()

    def ready(c, s):
        give(c, s, 3).wait_recv()
        for k in range(3):
            over(c, s, k).wait_recv()

    share0 = functools.partial(share, 0)
    share1 = functools.partial(share, 1)

    each(1, 8, lambda s: ring(s).start())
    cross(0).start()
    for k in range(4):
        give(0, 0, k).start()
    each(1, 3, hop)
    forward(0)
    share0(0)
    each(3, 8, hop)
    each(1, 3, forward)
    each(1, 3, share0)
    share1(0)
    each(3, 5, forward)
    each(3, 5, share0)
    each(5, 8, forward)
    each(5, 8, share0)
    each(1, 3, share1)
    load.wait()

    def logits(p):
        c, s0 = p // 2, lax.rem(p, 2) * 4
        each(s0, s0 + 4, lambda s: ready(c, s))
        side = xh + c * (1 - 2 * xh)
        part = side * 2 + lax.rem(p, 2)
        gf = G[side, :, pl.ds(s0, 4)].reshape(256, 1024).astype(F32)
        bias = jnp.sum(gf * gf, axis=1, keepdims=True) * (LOG2E / 32.0)

        def tile(i):
            g = G[side, :, pl.ds(s0, 4)].reshape(256, 1024)
            for u in range(8):
                n = pl.ds(pl.multiple_of(i * 2048 + u * 256, 256), 256)
                dots = lax.dot_general(g, vec[n, :], NT, preferred_element_type=F32)
                logit = dots * (LOG2E / 16.0) - bias
                top = jnp.max(logit, axis=0, keepdims=True)
                e = jnp.exp2(logit - top)
                E[part, :, n] = e
                ms[part, :, n] = top
                ss[part, :, n] = jnp.sum(e, axis=0, keepdims=True)

        tile(0)
        each(jnp.where(p == 0, 3, jnp.where(p == 1, 5, 8)), jnp.where(p == 0, 5, 8), share1)

    each(0, 4, logits)

    tops = [ms[q] for q in range(4)]
    top = functools.reduce(jnp.maximum, tops)
    scales = [jnp.exp2(t - top) for t in tops]
    total = functools.reduce(jnp.add, [ss[q] * scales[q] for q in range(4)])
    for q in range(4):
        ms[q] = scales[q] / total

    def responsibilities(q, u):
        n = slice(u * 512, u * 512 + 512)
        for p in range(4):
            r = (E[p, q * 64 : q * 64 + 64, n] * ms[p, :, n]).astype(BF16)
            rows = slice(p * 64, p * 64 + 64)
            R[q, rows, n] = r
            rf = r.astype(F32)
            part = rf[:, 0:128] + rf[:, 128:256] + rf[:, 256:384] + rf[:, 384:512]
            wp[q, rows, :] = part if u == 0 else wp[q, rows, :] + part

    for u in range(4):
        responsibilities(0, u)

    def lane_sums(k):
        block = wp[k // 2, pl.ds(pl.multiple_of(lax.rem(k, 2) * 128, 128), 128), :]
        W0[pl.ds(k, 1), :] = jnp.sum(block.T, axis=0, keepdims=True)

    def w_sib():
        return remote(W0, WS, ws, wr, 0, sibling)

    def w_a(j):
        return remote(W1, WA.at[j - 1], ws, wr, j, on_a(j))

    def w_b(j):
        return remote(W2, WB.at[j - 1], ws, wr, 3 + j, on_b(j))

    def w_z(s):
        return remote(W3, WZ.at[s - 1], ws, wr, 6 + s, on_z(distance(s)))

    a = jnp.where(first, y, x)
    b = jnp.where(first, x, y)

    def to_sib(q):
        return remote(SIB.at[q], RSIB.at[q], cs, cr, q, sibling)

    def to_a(q, j):
        return remote(SB.at[q, lax.rem(a + j, 4)], RB.at[q, j - 1], a_s, a_r, q * 3 + j - 1, on_a(j))

    def to_b(q, j):
        return remote(SB2.at[q, lax.rem(b + j, 4)], R2.at[q, j - 1], b_s, b_r, q * 3 + j - 1, on_b(j))

    def to_z(i, s):
        part = pl.ds(3, 1) if i else pl.ds(0, 3)
        return remote(S3.at[part, s], R3.at[s - 1, part], zs, zr, i * 7 + s - 1, on_z(distance(s)))

    lo = lax.broadcasted_iota(jnp.int32, (64, 128), 1) < 64

    def combine(q):
        to_sib(q).wait_recv()

        def column(yy):
            for xx in range(4):
                t = NUM[q, xx * 4 + yy] + RSIB[q, yy, xx].astype(F32)
                NUM[q, xx * 4 + yy] = t
                SB[q, jnp.where(first, yy, xx), jnp.where(first, xx, yy)] = t.astype(BF16)

        each(0, 4, column)
        for j in (1, 2, 3):
            to_a(q, j).start()

    for q in range(4):
        for yy in range(4):
            d = jnp.dot(R[q], vec[:, yy * 256 : yy * 256 + 256], preferred_element_type=F32)
            if q < 3:
                responsibilities(q + 1, yy)
            d = d.reshape(2, 8, 2, 8, 256)
            for xx in range(4):
                lanes = slice((xx % 2) * 128, (xx % 2) * 128 + 128)
                top_rows = d[xx // 2, :, 0, :, lanes].reshape(64, 128)
                low_rows = d[xx // 2, :, 1, :, lanes].reshape(64, 128)
                p0 = jnp.where(lo, top_rows, pltpu.roll(low_rows, 64, 1))
                p1 = jnp.where(lo, pltpu.roll(top_rows, 64, 1), low_rows)
                NUM[q, xx * 4 + yy] = jnp.where(first, p0, p1)
                SIB[q, yy, xx] = jnp.where(first, p1, p0).astype(BF16)
        to_sib(q).start()
        if q >= 1:
            combine(q - 1)
    each(0, 8, lane_sums)
    w_sib().start()
    combine(3)
    w_sib().wait_recv()
    W1[...] = W0[...] + WS[...]
    for j in (1, 2, 3):
        w_a(j).start()

    def second(q):
        for j in (1, 2, 3):
            to_a(q, j).wait_recv()
        for i in range(4):
            t = NUM[q, jnp.where(first, i * 4 + y, x * 4 + i)]
            for j in range(3):
                t = t + RB[q, j, i].astype(F32)
            S2[q, i] = t
            SB2[q, i] = t.astype(BF16)
        for j in (1, 2, 3):
            to_b(q, j).start()

    def third(i):
        def collect(q):
            for j in (1, 2, 3):
                to_b(q, j).wait_recv()
            t = S2[q, b]
            for j in range(3):
                t = t + R2[q, j].astype(F32)
            S3[q] = t.reshape(8, 8, 128)

        each(3 if i else 0, 4 if i else 3, collect)
        each(1, 8, lambda s: to_z(i, s).start())

    each(0, 3, second)
    for j in (1, 2, 3):
        w_a(j).wait_recv()
    W2[...] = W1[...] + WA[0] + WA[1] + WA[2]
    for j in (1, 2, 3):
        w_b(j).start()
    second(3)
    third(0)
    for j in (1, 2, 3):
        w_b(j).wait_recv()
    W3[...] = W2[...] + WB[0] + WB[1] + WB[2]
    each(1, 8, lambda s: w_z(s).start())
    third(1)

    each(1, 8, lambda s: w_z(s).wait_recv())
    weights = W3[...]
    for s in range(1, 8):
        weights = weights + pltpu.roll(WZ[s - 1], 128 - s * 16, 1)
    row = lax.broadcasted_iota(jnp.int32, (16, 128), 0)
    lane = lax.broadcasted_iota(jnp.int32, (16, 128), 1)
    mask = lane == row
    tile = pl.ds(pl.multiple_of((y * 2 + x_lo) * 128, 128), 128)
    load_cen.wait()
    block = cen[:, tile].astype(F32)
    block = jnp.where(first, block, pltpu.roll(block, 64, 1))

    def arrived(s):
        to_z(0, s).wait_recv()
        to_z(1, s).wait_recv()

    each(1, 8, arrived)
    for q in range(4):
        w = jnp.where(xh == 0, weights[2 * q : 2 * q + 1, :], weights[2 * q + 1 : 2 * q + 2, :])
        w = jnp.sum(jnp.where(mask, jnp.broadcast_to(w, (16, 128)), 0.0), axis=1, keepdims=True)
        f = S3[q, 0]
        for s in range(7):
            f = f + R3[s, q]
        rows = jnp.concatenate([f, pltpu.roll(f, 64, 1)], axis=0)
        res = (rows + block[q * 16 : q * 16 + 16]) / (w + 1.0)
        out[q * 16 : q * 16 + 16, :] = res[:, 0:64]

    def sent_pieces(s):
        cross(s).wait_send()
        for c in range(2):
            for k in range(4):
                give(c, s, k).wait_send()
            for k in range(3):
                over(c, s, k).wait_send()

    def sent_sums(q):
        to_sib(q).wait_send()
        for j in (1, 2, 3):
            to_a(q, j).wait_send()
            to_b(q, j).wait_send()

    def sent_z(s):
        ring(s).wait_send()
        to_z(0, s).wait_send()
        to_z(1, s).wait_send()
        w_z(s).wait_send()

    each(0, 8, sent_pieces)
    each(0, 4, sent_sums)
    each(1, 8, sent_z)
    w_sib().wait_send()
    for j in (1, 2, 3):
        w_a(j).wait_send()
        w_b(j).wait_send()


def per_device(vectors, centroids):
    dma = pltpu.SemaphoreType.DMA
    vmem = pltpu.VMEM
    return pl.pallas_call(
        kernel,
        out_shape=jax.ShapeDtypeStruct((64, 64), F32),
        in_specs=[pl.BlockSpec(memory_space=pl.ANY)] * 2,
        out_specs=pl.BlockSpec(memory_space=pltpu.VMEM),
        scratch_shapes=[
            vmem((2048, 1024), BF16),
            vmem((64, 1024), BF16),
            vmem((2, 4, 8, 16, 1024), BF16),
            vmem((4, 256, 2048), F32),
            vmem((4, 256, 2048), BF16),
            vmem((4, 1, 2048), F32),
            vmem((4, 1, 2048), F32),
            vmem((4, 256, 128), F32),
            vmem((4, 16, 64, 128), F32),
            vmem((4, 4, 4, 64, 128), BF16),
            vmem((4, 4, 4, 64, 128), BF16),
            vmem((4, 4, 4, 64, 128), BF16),
            vmem((4, 3, 4, 64, 128), BF16),
            vmem((4, 4, 64, 128), F32),
            vmem((4, 4, 64, 128), BF16),
            vmem((4, 3, 64, 128), BF16),
            vmem((4, 8, 8, 128), F32),
            vmem((7, 4, 8, 128), F32),
            vmem((8, 128), F32),
            vmem((8, 128), F32),
            vmem((8, 128), F32),
            vmem((8, 128), F32),
            vmem((8, 128), F32),
            vmem((3, 8, 128), F32),
            vmem((3, 8, 128), F32),
            vmem((7, 8, 128), F32),
            dma((3,)),
            dma((16,)), dma((16,)),
            dma((64,)), dma((64,)),
            dma((48,)), dma((48,)),
            dma((4,)), dma((4,)),
            dma((12,)), dma((12,)),
            dma((12,)), dma((12,)),
            dma((14,)), dma((14,)),
            dma((14,)), dma((14,)),
        ],
        compiler_params=pltpu.CompilerParams(
            collective_id=0, has_side_effects=True, vmem_limit_bytes=56 * 2**20
        ),
        name="step",
    )(vectors, centroids)


def solution(mesh):
    in_specs = (P(("dp", "cent"), None), P("cent", None))
    out_specs = P("cent", "dp")
    return jax.shard_map(
        per_device, mesh=mesh, in_specs=in_specs, out_specs=out_specs, check_vma=False
    )
```

time: 56.6 us -> 53.3 us (0.942)
  Pallas kernels: 55 us -> 51.4 us
    pallas_call x1, Pallas kernels: 55 us -> 51.4 us  [per_device(): pl.pallas_call(kernel, out_shape=jax.ShapeDtypeStruct((64, 64), F32), in_...]
where the time goes in v2:
time: 53.3 us; the launch traced here: 52.8 us
  Pallas kernels  51.4 us (96%)
  local copies, waits for them, and re-layouts  1.38 us (3%)
    pallas_call x1, Pallas kernels, per_device(): pl.pallas_call(kernel, out_shape=jax.ShapeDtypeStruct((64, 64), F32), in_...  51.4 us
    unnamed x1, local copies, waits for them, and re-layouts  1.38 us

profile of v2, /device:TPU:1, one launch (start us, length us, event | category | flops | bytes accessed | tf_op | source)
XLA Modules:
  0.0 52.8 jit_solution(10742786513048935297)
XLA Ops:
  0.0 51.4 %step.1 = f32[64,64]{1,0:T(8,128)} custom-call(bf16[2048,1024]{1,0:T(8,128)(2,1)} %vec_hbm.1, bf16[64,1024]{1,0:T(8,128)(2,1)} %cen_hbm.1), custom_call_target="tpu_custom_call" | custom-call | tf_op jit(solution)/shard_map/step/pallas_call | solution.py:368
  51.4 1.4 %copy.4 = f32[64,64]{1,0:T(8,128)} copy(f32[64,64]{1,0:T(8,128)} %step.1) | data formatting | bytes 32768

commit v3 on v2

--- a/solution.py
+++ b/solution.py
@@ -11,7 +11,6 @@
 F32 = jnp.float32
 BF16 = jnp.bfloat16
 LOG2E = math.log2(math.e)
-NT = (((1,), (1,)), ((), ()))
 
 
 def device(x, y, z, core):
@@ -28,7 +27,7 @@
 
 def kernel(
     vec_hbm, cen_hbm, out,
-    vec, cen, G, E, R, ms, ss, wp, NUM, SIB, RSIB, SB, RB, S2, SB2, R2, S3, R3,
+    vec, vecT, cen, G, E, R, ms, ss, wp, NUM, SIB, RSIB, SB, RB, S2, SB2, R2, S3, R3,
     W0, W1, W2, W3, WS, WA, WB, WZ,
     load_sem, gs, gr, fs, fr, hs, hr, cs, cr, a_s, a_r, b_s, b_r, zs, zr, ws, wr,
 ):
@@ -137,19 +136,24 @@
     cross(0).start()
     for k in range(4):
         give(0, 0, k).start()
+    load.wait()
+
+    def turn(i):
+        n = pl.ds(pl.multiple_of(i * 256, 256), 256)
+        vecT[:, n] = vec[n, :].T
+
+    each(0, 8, turn)
     each(1, 3, hop)
     forward(0)
+    each(3, 8, hop)
     share0(0)
-    each(3, 8, hop)
     each(1, 3, forward)
     each(1, 3, share0)
-    share1(0)
     each(3, 5, forward)
     each(3, 5, share0)
     each(5, 8, forward)
     each(5, 8, share0)
-    each(1, 3, share1)
-    load.wait()
+    each(0, 3, share1)
 
     def logits(p):
         c, s0 = p // 2, lax.rem(p, 2) * 4
@@ -163,7 +167,7 @@
             g = G[side, :, pl.ds(s0, 4)].reshape(256, 1024)
             for u in range(8):
                 n = pl.ds(pl.multiple_of(i * 2048 + u * 256, 256), 256)
-                dots = lax.dot_general(g, vec[n, :], NT, preferred_element_type=F32)
+                dots = jnp.dot(g, vecT[:, n], preferred_element_type=F32)
                 logit = dots * (LOG2E / 16.0) - bias
                 top = jnp.max(logit, axis=0, keepdims=True)
                 e = jnp.exp2(logit - top)
@@ -292,6 +296,18 @@
         each(3 if i else 0, 4 if i else 3, collect)
         each(1, 8, lambda s: to_z(i, s).start())
 
+    def sent_pieces(s):
+        cross(s).wait_send()
+        for c in range(2):
+            for k in range(4):
+                give(c, s, k).wait_send()
+            for k in range(3):
+                over(c, s, k).wait_send()
+
+    each(0, 8, sent_pieces)
+    each(1, 8, lambda s: ring(s).wait_send())
+    each(0, 4, lambda q: to_sib(q).wait_send())
+    w_sib().wait_send()
     each(0, 3, second)
     for j in (1, 2, 3):
         w_a(j).wait_recv()
@@ -300,6 +316,19 @@
         w_b(j).start()
     second(3)
     third(0)
+
+    def sent_a(q):
+        for j in (1, 2, 3):
+            to_a(q, j).wait_send()
+
+    def sent_b(q):
+        for j in (1, 2, 3):
+            to_b(q, j).wait_send()
+
+    each(0, 4, sent_a)
+    each(0, 3, sent_b)
+    for j in (1, 2, 3):
+        w_a(j).wait_send()
     for j in (1, 2, 3):
         w_b(j).wait_recv()
     W3[...] = W2[...] + WB[0] + WB[1] + WB[2]
@@ -318,47 +347,33 @@
     block = cen[:, tile].astype(F32)
     block = jnp.where(first, block, pltpu.roll(block, 64, 1))
 
+    divisors = []
+    for q in range(4):
+        w = jnp.where(xh == 0, weights[2 * q : 2 * q + 1, :], weights[2 * q + 1 : 2 * q + 2, :])
+        w = jnp.sum(jnp.where(mask, jnp.broadcast_to(w, (16, 128)), 0.0), axis=1, keepdims=True)
+        divisors.append(w + 1.0)
+
     def arrived(s):
         to_z(0, s).wait_recv()
         to_z(1, s).wait_recv()
 
     each(1, 8, arrived)
     for q in range(4):
-        w = jnp.where(xh == 0, weights[2 * q : 2 * q + 1, :], weights[2 * q + 1 : 2 * q + 2, :])
-        w = jnp.sum(jnp.where(mask, jnp.broadcast_to(w, (16, 128)), 0.0), axis=1, keepdims=True)
         f = S3[q, 0]
         for s in range(7):
             f = f + R3[s, q]
         rows = jnp.concatenate([f, pltpu.roll(f, 64, 1)], axis=0)
-        res = (rows + block[q * 16 : q * 16 + 16]) / (w + 1.0)
+        res = (rows + block[q * 16 : q * 16 + 16]) / divisors[q]
         out[q * 16 : q * 16 + 16, :] = res[:, 0:64]
 
-    def sent_pieces(s):
-        cross(s).wait_send()
-        for c in range(2):
-            for k in range(4):
-                give(c, s, k).wait_send()
-            for k in range(3):
-                over(c, s, k).wait_send()
-
-    def sent_sums(q):
-        to_sib(q).wait_send()
-        for j in (1, 2, 3):
-            to_a(q, j).wait_send()
-            to_b(q, j).wait_send()
-
     def sent_z(s):
-        ring(s).wait_send()
         to_z(0, s).wait_send()
         to_z(1, s).wait_send()
         w_z(s).wait_send()
 
-    each(0, 8, sent_pieces)
-    each(0, 4, sent_sums)
     each(1, 8, sent_z)
-    w_sib().wait_send()
-    for j in (1, 2, 3):
-        w_a(j).wait_send()
+    for j in (1, 2, 3):
+        to_b(3, j).wait_send()
         w_b(j).wait_send()
 
 
@@ -372,6 +387,7 @@
         out_specs=pl.BlockSpec(memory_space=pltpu.VMEM),
         scratch_shapes=[
             vmem((2048, 1024), BF16),
+            vmem((1024, 2048), BF16),
             vmem((64, 1024), BF16),
             vmem((2, 4, 8, 16, 1024), BF16),
             vmem((4, 256, 2048), F32),

time: 53.3 us -> 52.9 us (level)
  Pallas kernels: 51.4 us -> 50.5 us
    pallas_call x1, Pallas kernels: 51.4 us -> 50.5 us  [per_device(): pl.pallas_call(kernel, out_shape=jax.ShapeDtypeStruct((64, 64), F32), in_...]
where the time goes in v3:
time: 52.9 us; the launch traced here: 51.9 us
  Pallas kernels  50.5 us (95%)
  local copies, waits for them, and re-layouts  1.38 us (3%)
    pallas_call x1, Pallas kernels, per_device(): pl.pallas_call(kernel, out_shape=jax.ShapeDtypeStruct((64, 64), F32), in_...  50.5 us
    unnamed x1, local copies, waits for them, and re-layouts  1.38 us

profile of v3, /device:TPU:1, one launch (start us, length us, event | category | flops | bytes accessed | tf_op | source)
XLA Modules:
  0.0 51.9 jit_solution(18050065896744621906)
XLA Ops:
  0.0 50.5 %step.1 = f32[64,64]{1,0:T(8,128)} custom-call(bf16[2048,1024]{1,0:T(8,128)(2,1)} %vec_hbm.1, bf16[64,1024]{1,0:T(8,128)(2,1)} %cen_hbm.1), custom_call_target="tpu_custom_call" | custom-call | tf_op jit(solution)/shard_map/step/pallas_call | solution.py:383
  50.5 1.4 %copy.4 = f32[64,64]{1,0:T(8,128)} copy(f32[64,64]{1,0:T(8,128)} %step.1) | data formatting | bytes 32768

commit v4 on v3

--- a/solution.py
+++ b/solution.py
@@ -243,8 +243,9 @@
                 NUM[q, xx * 4 + yy] = t
                 SB[q, jnp.where(first, yy, xx), jnp.where(first, xx, yy)] = t.astype(BF16)
 
-        each(0, 4, column)
-        for j in (1, 2, 3):
+        for yy in range(4):
+            column(yy)
+        for j in (2, 1, 3):
             to_a(q, j).start()
 
     for q in range(4):
@@ -281,7 +282,7 @@
                 t = t + RB[q, j, i].astype(F32)
             S2[q, i] = t
             SB2[q, i] = t.astype(BF16)
-        for j in (1, 2, 3):
+        for j in (2, 1, 3):
             to_b(q, j).start()
 
     def third(i):
@@ -294,7 +295,7 @@
             S3[q] = t.reshape(8, 8, 128)
 
         each(3 if i else 0, 4 if i else 3, collect)
-        each(1, 8, lambda s: to_z(i, s).start())
+        each(1, 8, lambda s: to_z(i, 8 - s).start())
 
     def sent_pieces(s):
         cross(s).wait_send()

time: 52.9 us -> 52.6 us (level)
  no operation moved by 1% of the time
where the time goes in v4:
time: 52.6 us; the launch traced here: 51.7 us
  Pallas kernels  50.3 us (96%)
  local copies, waits for them, and re-layouts  1.38 us (3%)
    pallas_call x1, Pallas kernels, per_device(): pl.pallas_call(kernel, out_shape=jax.ShapeDtypeStruct((64, 64), F32), in_...  50.3 us
    unnamed x1, local copies, waits for them, and re-layouts  1.38 us

profile of v4, /device:TPU:1, one launch (start us, length us, event | category | flops | bytes accessed | tf_op | source)
XLA Modules:
  0.0 51.7 jit_solution(2629555285987060916)
XLA Ops:
  0.0 50.3 %step.1 = f32[64,64]{1,0:T(8,128)} custom-call(bf16[2048,1024]{1,0:T(8,128)(2,1)} %vec_hbm.1, bf16[64,1024]{1,0:T(8,128)(2,1)} %cen_hbm.1), custom_call_target="tpu_custom_call" | custom-call | tf_op jit(solution)/shard_map/step/pallas_call | solution.py:384
  50.4 1.4 %copy.4 = f32[64,64]{1,0:T(8,128)} copy(f32[64,64]{1,0:T(8,128)} %step.1) | data formatting | bytes 32768
